TPU v7x, 32 devices: a whole 2x2x4 slice. The times are simulated.
32 devices in a mesh: grp: 2 (over x), leaf: 8 (over z, y), sub: 2 (over core).
Axes of the slice: x: 2, y: 2, z: 4, core: 2. Of those that a mesh axis runs over, the one named last changes fastest.
Arguments:
- right_side: float32 [512, 2048], P(('grp', 'leaf', 'sub')), parts along dimension 0, may hold values from -24 to 24, as said below
- first_guess: float32 [512, 2048], P(('grp', 'leaf', 'sub')), parts along dimension 0, may hold values from -3 to 3
- couple: bfloat16 [512, 64, 384], P(('grp', 'leaf', 'sub')), parts along dimension 0, may hold values from -0.75 to 0.75
- send_lists: int32 [32, 2, 4], P(('grp', 'leaf', 'sub')), parts along dimension 0, may hold values from -1 to 15, as said below
- neighbours: int32 [512, 6], P(('grp', 'leaf', 'sub')), parts along dimension 0, may hold values from -1 to 23, as said below
Outputs:
- solution: float32 [512, 2048], P(('grp', 'leaf', 'sub')), parts along dimension 0
- residual: float32 [512, 2048], P(('grp', 'leaf', 'sub')), parts along dimension 0
There are 2 independent parts, one for each index of `grp`. A program takes and returns all parts, laid end to end along the dimension named above; each array names one. Nothing has to cross between parts.
Inputs may be any that keep to these rules, and one draw needn't show every extreme that they name: `right_side`: rows rise in scale along the element order. `send_lists`: for device d of a part and direction 0 (toward device d + 1) or 1 (toward device d - 1): distinct local element indices in the live slots, which come first, and -1 after them. The first device sends nothing in direction 1, the last nothing in direction 0; some device fills all 4 slots in direction 0 and the device after it all 4 in direction 1. `neighbours`: positions below 16 are the device's own elements, 16 + s the live slot s received from the previous device, 20 + s the live slot s received from the next device; -1 marks a face on the band's boundary.
All inputs are finite; a program needn't handle non-finite values.
Results may differ from a plain program's by a relative error of at most 0.034.
Values may be sent and summed in bfloat16 or wider, within the bound.
A program may use at most 64 MiB of HBM per device.

v0:
```python
import functools

import jax
import jax.numpy as jnp
from jax import lax
from jax.experimental import pallas as pl
from jax.experimental.pallas import tpu as pltpu
from jax.sharding import PartitionSpec as P

DOF = 64
FACES = 6
RHS = 32
SSTEP = 3
CYCLES = 4
KEPT = SSTEP * RHS
WIDTH = KEPT + RHS
MESH = pl.DeviceIdType.MESH


def gauss_jordan(system):
    tile = 8
    tiles = [system[first : first + tile] for first in range(0, KEPT, tile)]
    rows = lax.broadcasted_iota(jnp.int32, (tile, WIDTH), 0)

    def columns(value, at):
        first = at * tile
        return [
            jnp.broadcast_to(value[:, first + k : first + k + 1], (tile, WIDTH))
            for k in range(tile)
        ]

    for at in range(len(tiles)):
        block, factors = tiles[at], columns(tiles[at], at)
        outside = [columns(value, at) if i != at else None for i, value in enumerate(tiles)]
        for k in range(tile):
            inverse = 1.0 / factors[k][k : k + 1, :]

            def eliminated(value):
                pivot_row = value[k : k + 1, :] * inverse
                return jnp.where(rows == k, pivot_row, value - factors[k] * pivot_row)

            block = eliminated(block)
            factors = factors[: k + 1] + [eliminated(value) for value in factors[k + 1 :]]
        tiles[at] = block
        for i in range(len(tiles)):
            if i != at:
                value = tiles[i]
                for k in range(tile):
                    value = value - outside[i][k] * block[k : k + 1, :]
                tiles[i] = value
    return jnp.concatenate(tiles, axis=0)[:, KEPT:]


def split(value):
    high = value.astype(jnp.bfloat16)
    return high, (value - high.astype(jnp.float32)).astype(jnp.bfloat16)


def kernel(
    leaves, subs, elems, slots,
    right_ref, guess_ref, couple_ref, lists_ref, near_ref,
    x_ref, r_ref,
    ext, basis, current, power_one, power_two, packed_out, packed_in, partial, arrived, total,
    halo_send, halo_recv, sum_send, sum_recv,
):
    count = leaves * subs
    share = WIDTH // count
    zero_at = elems + 2 * slots
    grp, leaf, sub = (lax.axis_index(name) for name in ("grp", "leaf", "sub"))
    me = leaf * subs + sub
    steps = [(far, near) for far in range(leaves) for near in range(subs)][1:]

    def turned(value, step, size):
        moved = value + step
        return jnp.where(moved >= size, moved - size, moved)

    def place(step):
        return (grp, turned(leaf, step[0], leaves), turned(sub, step[1], subs))

    def peer(step):
        return turned(leaf, step[0], leaves) * subs + turned(sub, step[1], subs)

    last_sub, first_sub = sub == subs - 1, sub == 0
    following = (
        grp, turned(leaf, jnp.where(last_sub, 1, 0), leaves), jnp.where(last_sub, 0, sub + 1)
    )
    preceding = (
        grp,
        turned(leaf, jnp.where(first_sub, leaves - 1, 0), leaves),
        jnp.where(first_sub, subs - 1, sub - 1),
    )

    barrier = pltpu.get_barrier_semaphore()
    for step in steps:
        pl.semaphore_signal(barrier, inc=1, device_id=place(step), device_id_type=MESH)
    pl.semaphore_wait(barrier, count - 1)

    for side in range(2):
        ext[side, elems:] = jnp.zeros((2 * slots + 1, DOF, RHS), jnp.bfloat16)

    def halo_copy(way, at, target):
        return pltpu.make_async_remote_copy(
            src_ref=packed_out.at[at, way],
            dst_ref=packed_in.at[at, way],
            send_sem=halo_send.at[at, way],
            recv_sem=halo_recv.at[at, way],
            device_id=target,
            device_id_type=MESH,
        )

    def exchange(side, at, meanwhile=None):
        def pack(way):
            blocks = []
            for slot in range(slots):
                listed = lists_ref[0, way, slot]
                blocks.append(ext[side, jnp.where(listed < 0, zero_at, listed)])
            packed_out[at, way] = jnp.concatenate(blocks, axis=1)

        ahead = halo_copy(0, at, following)
        back = halo_copy(1, at, preceding)
        has_next = me < count - 1
        has_previous = me > 0
        pack(0)

        @pl.when(has_next)
        def _():
            ahead.start()

        pack(1)

        @pl.when(has_previous)
        def _():
            back.start()

        if meanwhile is not None:
            meanwhile()

        @pl.when(has_previous)
        def _():
            ahead.wait_recv()
            for slot in range(slots):
                ext[side, elems + slot] = packed_in[at, 0, :, slot * RHS : (slot + 1) * RHS]

        @pl.when(has_next)
        def _():
            back.wait_recv()
            for slot in range(slots):
                ext[side, elems + slots + slot] = packed_in[at, 1, :, slot * RHS : (slot + 1) * RHS]

        @pl.when(has_next)
        def _():
            ahead.wait_send()

        @pl.when(has_previous)
        def _():
            back.wait_send()

    def applied(side, element):
        blocks = []
        for face in range(FACES):
            near = near_ref[element, face]
            blocks.append(ext[side, jnp.where(near < 0, zero_at, near)])
        gathered = jnp.concatenate(blocks, axis=0)
        return jnp.dot(couple_ref[element], gathered, preferred_element_type=jnp.float32)

    def rows_of(element):
        return slice(element * DOF, (element + 1) * DOF)

    def keep(rows, order, value):
        high, low = split(value)
        if order <= SSTEP:
            at, below = order * RHS, WIDTH + order * RHS
        else:
            at = 2 * WIDTH + (order - SSTEP - 1) * RHS
            below = at + 2 * RHS
        basis[rows, at : at + RHS] = high
        basis[rows, below : below + RHS] = low
        return high

    def advance(side, at, order, store, meanwhile=None):
        exchange(side, at, meanwhile)
        for element in range(elems):
            rows = rows_of(element)
            image = applied(side, element)
            keep(rows, order, current[rows, :] - image)
            if store:
                current[rows, :] = image
                ext[1 - side, element] = image.astype(jnp.bfloat16)

    for element in range(elems):
        guess = guess_ref[rows_of(element), :]
        x_ref[rows_of(element), :] = guess
        ext[1, element] = guess.astype(jnp.bfloat16)
    exchange(1, SSTEP)
    for element in range(elems):
        rows = rows_of(element)
        first = right_ref[rows, :] - guess_ref[rows, :] + applied(1, element)
        r_ref[rows, :] = first
        ext[0, element] = first.astype(jnp.bfloat16)

    exchange(0, 0)
    for element in range(elems):
        rows = rows_of(element)
        image = applied(0, element)
        power_one[rows, :] = image
        ext[1, element] = image.astype(jnp.bfloat16)
    exchange(1, 1)
    for element in range(elems):
        rows = rows_of(element)
        image = applied(1, element)
        power_two[rows, :] = image
        current[rows, :] = image
        ext[0, element] = image.astype(jnp.bfloat16)

    def sum_copy(source, target, step, phase):
        return pltpu.make_async_remote_copy(
            src_ref=source,
            dst_ref=target,
            send_sem=sum_send.at[phase],
            recv_sem=sum_recv.at[phase],
            device_id=place(step),
            device_id_type=MESH,
        )

    def refresh():
        for element in range(elems):
            rows = rows_of(element)
            zero, one, two = r_ref[rows, :], power_one[rows, :], power_two[rows, :]
            keep(rows, SSTEP, zero)
            keep(rows, 0, zero - one)
            keep(rows, 1, one - two)

    def cycle(repeat, carry):
        advance(0, 0, 2, True, refresh)
        products = lax.dot_general(
            basis[:, :WIDTH], basis[:, : 2 * WIDTH], (((0,), (0,)), ((), ())),
            preferred_element_type=jnp.float32,
        )
        cross = products[:, WIDTH:]
        gram = products[:, :WIDTH] + cross + cross.T
        for shard in range(count):
            partial[shard] = gram[shard * share : (shard + 1) * share, :]
        for slot, step in enumerate(steps):
            sum_copy(partial.at[peer(step)], arrived.at[slot + 1], step, 0).start()
        rest = pl.ds(1, count - 1)
        whole = sum_copy(partial.at[rest], arrived.at[rest], steps[0], 0)
        advance(1, 1, 4, True)
        whole.wait_recv()
        reduced = partial[me]
        for step in range(1, count):
            reduced = reduced + arrived[step]
        total[me] = reduced
        for step in steps:
            sum_copy(total.at[me], total.at[me], step, 1).start()
        whole.wait_send()
        both = sum_copy(total.at[rest], total.at[rest], steps[0], 1)
        advance(0, 2, 5, False)
        both.wait_recv()
        both.wait_send()
        system = jnp.concatenate(
            [total[shard] for shard in range(count)], axis=0
        )[:KEPT]
        coeffs = gauss_jordan(system)

        c0, c1, c2 = coeffs[:RHS], coeffs[RHS : 2 * RHS], coeffs[2 * RHS :]
        nothing = jnp.zeros((RHS, RHS), jnp.float32)
        late = c1 + c2
        factor = jnp.concatenate(
            [
                jnp.concatenate([c0, c1, c2, nothing, nothing, nothing], axis=0),
                jnp.concatenate([-late, -c2, nothing, c0 + late, nothing, nothing], axis=0),
                jnp.concatenate([nothing, c0, c1, nothing, c2, nothing], axis=0),
                jnp.concatenate([nothing, nothing, c0, nothing, c1, c2], axis=0),
            ],
            axis=1,
        )
        high, low = split(factor)
        left = jnp.concatenate([high[:WIDTH], high[:WIDTH], high[WIDTH:], high[WIDTH:]], axis=0)
        right = jnp.concatenate(
            [low[:WIDTH], jnp.zeros_like(low[:WIDTH]), low[WIDTH:], jnp.zeros_like(low[WIDTH:])],
            axis=0,
        )
        factor = jnp.concatenate([left, right], axis=1)
        for element in range(elems):
            rows = rows_of(element)
            change = jnp.dot(basis[rows, :], factor, preferred_element_type=jnp.float32)
            change = change[:, :WIDTH] + change[:, WIDTH:]
            x_ref[rows, :] = x_ref[rows, :] + change[:, RHS : 2 * RHS]
            later = r_ref[rows, :] - change[:, :RHS]
            one = power_one[rows, :] - change[:, 2 * RHS : 3 * RHS]
            two = power_two[rows, :] - change[:, 3 * RHS :]
            r_ref[rows, :] = later
            power_one[rows, :] = one
            power_two[rows, :] = two
            current[rows, :] = two
            ext[0, element] = two.astype(jnp.bfloat16)
        return carry

    lax.fori_loop(0, CYCLES, cycle, 0)


def shards(leaves, subs, right_side, first_guess, couple, send_lists, neighbours):
    elems, _, _ = couple.shape
    slots = send_lists.shape[2]
    count = leaves * subs
    share = WIDTH // count
    rows = elems * DOF
    vmem = pl.BlockSpec(memory_space=pltpu.VMEM)
    smem = pl.BlockSpec(memory_space=pltpu.SMEM)
    field = jax.ShapeDtypeStruct((rows, RHS), jnp.float32)
    x, r = pl.pallas_call(
        functools.partial(kernel, leaves, subs, elems, slots),
        out_shape=(field, field),
        in_specs=[vmem, vmem, vmem, smem, smem],
        out_specs=(vmem, vmem),
        scratch_shapes=[
            pltpu.VMEM((2, elems + 2 * slots + 1, DOF, RHS), jnp.bfloat16),
            pltpu.VMEM((rows, 2 * WIDTH + 4 * RHS), jnp.bfloat16),
            pltpu.VMEM((rows, RHS), jnp.float32),
            pltpu.VMEM((rows, RHS), jnp.float32),
            pltpu.VMEM((rows, RHS), jnp.float32),
            pltpu.VMEM((SSTEP + 1, 2, DOF, slots * RHS), jnp.bfloat16),
            pltpu.VMEM((SSTEP + 1, 2, DOF, slots * RHS), jnp.bfloat16),
            pltpu.VMEM((count, share, WIDTH), jnp.float32),
            pltpu.VMEM((count, share, WIDTH), jnp.float32),
            pltpu.VMEM((count, share, WIDTH), jnp.float32),
            pltpu.SemaphoreType.DMA((SSTEP + 1, 2)),
            pltpu.SemaphoreType.DMA((SSTEP + 1, 2)),
            pltpu.SemaphoreType.DMA((2,)),
            pltpu.SemaphoreType.DMA((2,)),
        ],
        compiler_params=pltpu.CompilerParams(
            collective_id=0, has_side_effects=True, vmem_limit_bytes=40 * 1024 * 1024
        ),
    )(
        right_side.reshape(rows, RHS), first_guess.reshape(rows, RHS),
        couple, send_lists, neighbours,
    )
    return x.reshape(right_side.shape), r.reshape(right_side.shape)


def solution(mesh):
    lead = ("grp", "leaf", "sub")
    flat, deep = P(lead, None), P(lead, None, None)
    return jax.shard_map(
        functools.partial(shards, mesh.shape["leaf"], mesh.shape["sub"]),
        mesh=mesh,
        in_specs=(flat, flat, deep, deep, flat),
        out_specs=(flat, flat),
        check_vma=False,
    )
```

profile of v0, /device:TPU:0, one launch (start us, length us, event | category | flops | bytes accessed | tf_op | source)
XLA Modules:
  0.0 104.0 jit_solution(10545897558632296212)
XLA Ops:
  0.6 0.0 copy-start
  0.6 0.8 copy.8.near_ref
  1.5 1.1 %reshape.16.right_ref = f32[1024,32]{1,0:T(8,128)S(1)} reshape(f32[16,2048]{1,0:T(8,128)} %param.5) | data formatting | bytes 262144 | tf_op jit(solution)/shard_map/reshape | solution.py:336
  2.6 0.0 copy-start.1
  2.6 1.1 %reshape.17.guess_ref = f32[1024,32]{1,0:T(8,128)S(1)} reshape(f32[16,2048]{1,0:T(8,128)} %param.6) | data formatting | bytes 262144 | tf_op jit(solution)/shard_map/reshape | solution.py:336
  3.7 0.0 copy-done
  3.7 0.0 copy-done.1
  3.7 98.5 %shard_map.68 = (f32[1024,32]{1,0:T(8,128)S(1)}, f32[1024,32]{1,0:T(8,128)S(1)}) custom-call(f32[1024,32]{1,0:T(8,128)S(1)} %reshape.16.right_ref, f32[1024,32]{1,0:T(8,128)S(1)} %reshape.17.guess_ref, bf16[16,64,384]{2,1,0:T(8,128)(2,1)S(1)} %copy-done, s32[1,2,4]{2,1,0:T(2,128)S(1)} %copy-done.1, s32[16,6]{1,0:T(8,128)S(1)} %copy.8.near_ref), custom_call_target="tpu_custom_call" | custom-call | tf_op jit(solution)/shard_map/pallas_call | solution.py:311
  102.2 0.9 reshape.18
  103.1 0.9 reshape.19
Async XLA Ops:
  0.6 3.0 %copy-start = (bf16[16,64,384]{2,1,0:T(8,128)(2,1)S(1)}, bf16[16,64,384]{2,1,0:T(8,128)(2,1)}, u32[]{:S(2)}) copy-start(bf16[16,64,384]{2,1,0:T(8,128)(2,1)} %couple_ref.1) | copy-start | bytes 2359300
  2.6 1.1 %copy-start.1 = (s32[1,2,4]{2,1,0:T(2,128)S(1)}, s32[1,2,4]{2,1,0:T(2,128)}, u32[]{:S(2)}) copy-start(s32[1,2,4]{2,1,0:T(2,128)} %lists_ref.1) | copy-start | bytes 100
where the time goes:
time: 104 us
  Pallas kernels  98.5 us (95%)
  local copies, waits for them, and re-layouts  4.77 us (5%)
    pallas_call x1, Pallas kernels, shards(): pl.pallas_call(functools.partial(kernel, leaves, subs, elems, slots), out...  98.5 us

commit v1 on v0

v1 whole, which is shorter than its diff:
```python
import functools

import jax
import jax.numpy as jnp
from jax import lax
from jax.experimental import pallas as pl
from jax.experimental.pallas import tpu as pltpu
from jax.sharding import PartitionSpec as P

DOF = 64
FACES = 6
RHS = 32
SSTEP = 3
CYCLES = 4
KEPT = SSTEP * RHS
WIDTH = KEPT + RHS
MESH = pl.DeviceIdType.MESH


def gauss_jordan(system):
    tile = 8
    tiles = [system[first : first + tile] for first in range(0, KEPT, tile)]
    rows = lax.broadcasted_iota(jnp.int32, (tile, WIDTH), 0)

    def columns(value, at):
        first = at * tile
        return [
            jnp.broadcast_to(value[:, first + k : first + k + 1], (tile, WIDTH))
            for k in range(tile)
        ]

    for at in range(len(tiles)):
        block, factors = tiles[at], columns(tiles[at], at)
        outside = [columns(value, at) if i != at else None for i, value in enumerate(tiles)]
        for k in range(tile):
            inverse = 1.0 / factors[k][k : k + 1, :]

            def eliminated(value):
                pivot_row = value[k : k + 1, :] * inverse
                return jnp.where(rows == k, pivot_row, value - factors[k] * pivot_row)

            block = eliminated(block)
            factors = factors[: k + 1] + [eliminated(value) for value in factors[k + 1 :]]
        tiles[at] = block
        for i in range(len(tiles)):
            if i != at:
                value = tiles[i]
                for k in range(tile):
                    value = value - outside[i][k] * block[k : k + 1, :]
                tiles[i] = value
    return jnp.concatenate(tiles, axis=0)


def split(value):
    high = value.astype(jnp.bfloat16)
    return high, (value - high.astype(jnp.float32)).astype(jnp.bfloat16)


def kernel(
    leaves, subs, elems, slots,
    right_ref, guess_ref, couple_ref, lists_ref, near_ref,
    x_ref, r_ref,
    ext, powers, high_ref, low_ref, table, packed_out, packed_in, partial, arrived, total,
    halo_send, halo_recv, sum_send, sum_recv,
):
    count = leaves * subs
    share = WIDTH // count
    pairs, wings = elems // 2, slots // 2
    zero_at = elems + 2 * slots
    grp, leaf, sub = (lax.axis_index(name) for name in ("grp", "leaf", "sub"))
    me = leaf * subs + sub
    steps = [(far, near) for far in range(leaves) for near in range(subs)][1:]

    def turned(value, step, size):
        moved = value + step
        return jnp.where(moved >= size, moved - size, moved)

    def place(step):
        return (grp, turned(leaf, step[0], leaves), turned(sub, step[1], subs))

    def peer(step):
        return turned(leaf, step[0], leaves) * subs + turned(sub, step[1], subs)

    last_sub, first_sub = sub == subs - 1, sub == 0
    following = (
        grp, turned(leaf, jnp.where(last_sub, 1, 0), leaves), jnp.where(last_sub, 0, sub + 1)
    )
    preceding = (
        grp,
        turned(leaf, jnp.where(first_sub, leaves - 1, 0), leaves),
        jnp.where(first_sub, subs - 1, sub - 1),
    )
    has_next = me < count - 1
    has_previous = me > 0

    barrier = pltpu.get_barrier_semaphore()
    for step in steps:
        pl.semaphore_signal(barrier, inc=1, device_id=place(step), device_id_type=MESH)

    half = lax.broadcasted_iota(jnp.int32, (RHS, 2 * DOF), 1) < DOF

    def swapped(value):
        return jnp.concatenate([value[:, DOF:], value[:, :DOF]], axis=1)

    def lanes(pair):
        return slice(pair * 2 * DOF, (pair + 1) * 2 * DOF)

    def put(side, pair, value):
        ext[side, 2 * pair] = value.astype(jnp.bfloat16)
        ext[side, 2 * pair + 1] = swapped(value).astype(jnp.bfloat16)

    for side in range(3):
        ext[side, elems:] = jnp.zeros((2 * slots + 2, RHS, 2 * DOF), jnp.bfloat16)
    tail = (WIDTH + SSTEP * RHS, 2 * WIDTH)
    high_ref[tail[0] : tail[1]] = jnp.zeros((tail[1] - tail[0], pairs * 2 * DOF), jnp.bfloat16)
    low_ref[tail[0] : tail[1]] = jnp.zeros((tail[1] - tail[0], pairs * 2 * DOF), jnp.bfloat16)
    for element in range(elems):
        for face in range(FACES):
            near = near_ref[face, element]
            at = jnp.where(near < 0, zero_at, near)
            table[element * FACES + face] = at if face % 2 == 0 else at ^ 1
    for way in range(2):
        for slot in range(slots):
            listed = lists_ref[0, way, slot]
            at = jnp.where(listed < 0, zero_at, listed)
            table[elems * FACES + way * slots + slot] = at if slot % 2 == 0 else at ^ 1
    for pair in range(pairs):
        guess = guess_ref[:, lanes(pair)]
        x_ref[:, lanes(pair)] = guess
        put(2, pair, guess)

    pl.semaphore_wait(barrier, count - 1)

    def halo_copy(way, side, target):
        return pltpu.make_async_remote_copy(
            src_ref=packed_out.at[side, way],
            dst_ref=packed_in.at[side, way],
            send_sem=halo_send.at[side, way],
            recv_sem=halo_recv.at[side, way],
            device_id=target,
            device_id_type=MESH,
        )

    def ahead(side):
        return halo_copy(0, side, following)

    def back(side):
        return halo_copy(1, side, preceding)

    def begin(side):
        def pack(way):
            for wing in range(wings):
                at = elems * FACES + way * slots + 2 * wing
                packed_out[side, way, wing] = jnp.where(
                    half, ext[side, table[at]], ext[side, table[at + 1]]
                )

        pack(0)

        @pl.when(has_next)
        def _():
            ahead(side).start()

        pack(1)

        @pl.when(has_previous)
        def _():
            back(side).start()

    def finish(side):
        @pl.when(has_previous)
        def _():
            ahead(side).wait_recv()
            for wing in range(wings):
                put(side, pairs + wing, packed_in[side, 0, wing].astype(jnp.float32))

        @pl.when(has_next)
        def _():
            back(side).wait_recv()
            for wing in range(wings):
                put(side, pairs + wings + wing, packed_in[side, 1, wing].astype(jnp.float32))

        @pl.when(has_next)
        def _():
            ahead(side).wait_send()

        @pl.when(has_previous)
        def _():
            back(side).wait_send()

    def applied(side, pair):
        def gathered(element):
            blocks = []
            for face in range(0, FACES, 2):
                at = element * FACES + face
                blocks.append(jnp.where(half, ext[side, table[at]], ext[side, table[at + 1]]))
            return jnp.concatenate(blocks, axis=1)

        both = jnp.concatenate([gathered(2 * pair), gathered(2 * pair + 1)], axis=0)
        image = lax.dot_general(
            both, couple_ref[lanes(pair), :], (((1,), (1,)), ((), ())),
            preferred_element_type=jnp.float32,
        )
        return jnp.where(half, image[:RHS], image[RHS:])

    def advance(side, order, store=True):
        for pair in range(pairs):
            image = applied(side, pair)
            powers[order, :, lanes(pair)] = image
            if store:
                put((side + 1) % 3, pair, image)

    def keep(block, value, at):
        rows = slice(block * RHS, (block + 1) * RHS)
        high_ref[rows, at], low_ref[rows, at] = split(value)

    def differ(block, order):
        for pair in range(pairs):
            at = lanes(pair)
            keep(block, powers[order, :, at] - powers[order + 1, :, at], at)

    last = 2 * SSTEP

    begin(2)
    finish(2)
    for pair in range(pairs):
        at = lanes(pair)
        first = right_ref[:, at] - guess_ref[:, at] + applied(2, pair)
        powers[0, :, at] = first
        put(0, pair, first)
    begin(0)
    for pair in range(pairs):
        keep(last, powers[0, :, lanes(pair)], lanes(pair))
    for order in range(SSTEP):
        finish(order)
        advance(order, order + 1)
        if order < SSTEP - 1:
            begin(order + 1)
        differ(order, order)

    def sum_copy(source, target, step, phase):
        return pltpu.make_async_remote_copy(
            src_ref=source,
            dst_ref=target,
            send_sem=sum_send.at[phase],
            recv_sem=sum_recv.at[phase],
            device_id=place(step),
            device_id_type=MESH,
        )

    rest = pl.ds(1, count - 1)

    def scatter():
        return sum_copy(partial.at[rest], arrived.at[rest], steps[0], 0)

    def gather():
        return sum_copy(total.at[rest], total.at[rest], steps[0], 1)

    def begin_sum():
        def stacked(ref):
            return jnp.concatenate([ref[:KEPT], ref[last * RHS : (last + 1) * RHS]], axis=0)

        def product(left, right):
            return lax.dot_general(
                left, right, (((1,), (1,)), ((), ())), preferred_element_type=jnp.float32
            )

        high, low = stacked(high_ref), stacked(low_ref)
        gram = product(high, high) + product(high, low) + product(low, high)
        for shard in range(count):
            partial[shard] = gram[shard * share : (shard + 1) * share, :]
        for slot, step in enumerate(steps):
            sum_copy(partial.at[peer(step)], arrived.at[slot + 1], step, 0).start()

    def turn_sum():
        scatter().wait_recv()
        reduced = partial[me]
        for step in range(1, count):
            reduced = reduced + arrived[step]
        total[me] = reduced
        for step in steps:
            sum_copy(total.at[me], total.at[me], step, 1).start()
        scatter().wait_send()

    def finish_sum():
        gather().wait_recv()
        gather().wait_send()

    def solved():
        system = jnp.concatenate([total[shard] for shard in range(count)], axis=0)[:KEPT]
        whole = gauss_jordan(system)
        whole = jnp.concatenate([whole, jnp.zeros((RHS, WIDTH), jnp.float32)], axis=0)
        return whole.T[KEPT:]

    lane = lax.broadcasted_iota(jnp.int32, (RHS, WIDTH), 1)

    def factors(coeffs, final):
        def rolled(by):
            by = by * RHS
            return jnp.concatenate([coeffs[:, WIDTH - by :], coeffs[:, : WIDTH - by]], axis=1)

        by_one, by_two, by_three = rolled(1), rolled(2), rolled(3)
        nothing = jnp.zeros_like(coeffs)

        def within(value, first, end):
            return jnp.where((lane >= first * RHS) & (lane < end * RHS), value, 0.0)

        rows = [
            (coeffs, nothing),
            (
                -within(by_three, 0, 2) - within(by_two, 0, 1),
                within(by_two + by_one + coeffs, 2, 3),
            ),
        ]
        if not final:
            rows += [
                (by_one, nothing),
                (within(by_two, 2, 4), within(by_two, 0, 1)),
                (within(by_three, 3, 4), within(by_three, 0, 2)),
            ]
        return split(
            jnp.concatenate([jnp.concatenate(row, axis=1) for row in rows], axis=0)
        )

    def changes(parts, at):
        high, low = high_ref[:, at], low_ref[:, at]
        return (
            jnp.dot(parts[0], high, preferred_element_type=jnp.float32)
            + jnp.dot(parts[0], low, preferred_element_type=jnp.float32)
            + jnp.dot(parts[1], high, preferred_element_type=jnp.float32)
        )

    spans = [slice(first * 2 * DOF, (first + 2) * 2 * DOF) for first in range(0, pairs, 2)]

    def cycle(repeat, carry):
        begin(0)
        begin_sum()
        finish(0)
        advance(0, SSTEP + 1)
        begin(1)
        differ(SSTEP, SSTEP)
        turn_sum()
        finish(1)
        advance(1, SSTEP + 2)
        begin(2)
        differ(SSTEP + 1, SSTEP + 1)
        finish_sum()
        finish(2)
        coeffs = solved()
        advance(2, SSTEP + 3, False)
        differ(SSTEP + 2, SSTEP + 2)
        parts = factors(coeffs, False)
        for index, at in enumerate(spans):
            change = changes(parts, at)
            x_ref[:, at] = x_ref[:, at] + change[RHS : 2 * RHS]
            fields = [powers[0, :, at] - change[:RHS]]
            for order in range(1, SSTEP + 1):
                rows = slice((order + 1) * RHS, (order + 2) * RHS)
                fields.append(powers[order, :, at] - change[rows])
            for order in range(SSTEP + 1):
                powers[order, :, at] = fields[order]
            for pair in range(2):
                put(0, 2 * index + pair, fields[SSTEP][:, lanes(pair)])
            keep(last, fields[0], at)
            for order in range(SSTEP):
                keep(order, fields[order] - fields[order + 1], at)
        return carry

    lax.fori_loop(0, CYCLES - 1, cycle, 0)
    begin_sum()
    turn_sum()
    finish_sum()
    parts = factors(solved(), True)
    for at in spans:
        change = changes(parts, at)
        x_ref[:, at] = x_ref[:, at] + change[RHS:]
        r_ref[:, at] = powers[0, :, at] - change[:RHS]


def shards(leaves, subs, right_side, first_guess, couple, send_lists, neighbours):
    elems, _, _ = couple.shape
    slots = send_lists.shape[2]
    count = leaves * subs
    share = WIDTH // count
    rows = elems * DOF
    vmem = pl.BlockSpec(memory_space=pltpu.VMEM)
    smem = pl.BlockSpec(memory_space=pltpu.SMEM)
    field = jax.ShapeDtypeStruct((RHS, rows), jnp.float32)

    def turned(value):
        return value.reshape(rows, RHS).T

    x, r = pl.pallas_call(
        functools.partial(kernel, leaves, subs, elems, slots),
        out_shape=(field, field),
        in_specs=[vmem, vmem, vmem, smem, smem],
        out_specs=(vmem, vmem),
        scratch_shapes=[
            pltpu.VMEM((3, elems + 2 * slots + 2, RHS, 2 * DOF), jnp.bfloat16),
            pltpu.VMEM((2 * SSTEP + 1, RHS, rows), jnp.float32),
            pltpu.VMEM((2 * WIDTH, rows), jnp.bfloat16),
            pltpu.VMEM((2 * WIDTH, rows), jnp.bfloat16),
            pltpu.SMEM((elems * FACES + 2 * slots,), jnp.int32),
            pltpu.VMEM((3, 2, slots // 2, RHS, 2 * DOF), jnp.bfloat16),
            pltpu.VMEM((3, 2, slots // 2, RHS, 2 * DOF), jnp.bfloat16),
            pltpu.VMEM((count, share, WIDTH), jnp.float32),
            pltpu.VMEM((count, share, WIDTH), jnp.float32),
            pltpu.VMEM((count, share, WIDTH), jnp.float32),
            pltpu.SemaphoreType.DMA((3, 2)),
            pltpu.SemaphoreType.DMA((3, 2)),
            pltpu.SemaphoreType.DMA((2,)),
            pltpu.SemaphoreType.DMA((2,)),
        ],
        compiler_params=pltpu.CompilerParams(
            collective_id=0, has_side_effects=True, vmem_limit_bytes=40 * 1024 * 1024
        ),
    )(
        turned(right_side), turned(first_guess),
        couple.reshape(rows, FACES * DOF), send_lists, neighbours.T,
    )
    return x.T.reshape(right_side.shape), r.T.reshape(right_side.shape)


def solution(mesh):
    lead = ("grp", "leaf", "sub")
    flat, deep = P(lead, None), P(lead, None, None)
    return jax.shard_map(
        functools.partial(shards, mesh.shape["leaf"], mesh.shape["sub"]),
        mesh=mesh,
        in_specs=(flat, flat, deep, deep, flat),
        out_specs=(flat, flat),
        check_vma=False,
    )
```

time: 104 us -> 87.3 us (0.84)
  Pallas kernels: 98.5 us -> 81.3 us
    pallas_call x1, Pallas kernels: 98.5 us -> 81.3 us  [shards(): pl.pallas_call(functools.partial(kernel, leaves, subs, elems, slots), out...]
    reshape x4 -> x6, local copies, waits for them, and re-layouts: 3.93 us -> 3.36 us  [the longest x2 1.79 us: shards(): return (x.T.reshape(right_side.shape), r.T.reshape(right_side.shape))]
where the time goes in v1:
time: 87.3 us; the launch traced here: 87.1 us
  Pallas kernels  81.3 us (93%)
  local copies, waits for them, and re-layouts  5.19 us (6%)
    pallas_call x1, Pallas kernels, shards(): pl.pallas_call(functools.partial(kernel, leaves, subs, elems, slots), out...  81.3 us
    reshape x2, local copies, waits for them, and re-layouts, shards(): return (x.T.reshape(right_side.shape), r.T.reshape(right_side.shape))  1.79 us

profile of v1, /device:TPU:0, one launch (start us, length us, event | category | flops | bytes accessed | tf_op | source)
XLA Modules:
  0.0 87.1 jit_solution(5518741905211570634)
XLA Ops:
  0.6 1.1 %reshape.19 = f32[1024,32]{1,0:T(8,128)S(1)} reshape(f32[16,2048]{1,0:T(8,128)} %param.5) | data formatting | bytes 262144 | tf_op jit(solution)/shard_map/reshape | solution.py:391
  1.7 0.0 copy-start.3
  1.7 0.2 copy.7
  1.9 0.0 copy-start
  1.9 0.7 copy-done.3
  2.6 0.2 reshape.20
  2.8 0.0 copy-start.1
  2.8 0.2 copy.8
  3.0 0.0 copy-start.2
  3.0 0.1 copy-done
  3.0 0.5 copy-done.1
  3.5 0.1 copy-done.2
  3.7 81.3 %shard_map.68 = (f32[32,1024]{1,0:T(8,128)S(1)}, f32[32,1024]{1,0:T(8,128)S(1)}) custom-call(f32[32,1024]{1,0:T(8,128)S(1)} %bitcast.7, f32[32,1024]{1,0:T(8,128)S(1)} %bitcast.8, bf16[1024,384]{1,0:T(8,128)(2,1)S(1)} %bitcast.6, s32[1,2,4]{2,1,0:T(2,128)S(1)} %copy-done.2, s32[6,16]{1,0:T(8,128)S(1)} %bitcast.11), custom_call_target="tpu_custom_call" | custom-call | tf_op jit(solution)/shard_map/pallas_call | solution.py:393
  84.9 0.2 copy.10
  85.1 0.9 %reshape.23 = f32[16,2048]{1,0:T(8,128)} reshape(f32[1024,32]{1,0:T(8,128)S(1)} %copy.10) | data formatting | bytes 262144 | tf_op jit(solution)/shard_map/reshape | solution.py:421
  86.0 0.2 copy.9
  86.2 0.9 %reshape.22 = f32[16,2048]{1,0:T(8,128)} reshape(f32[1024,32]{1,0:T(8,128)S(1)} %copy.9) | data formatting | bytes 262144 | tf_op jit(solution)/shard_map/reshape | solution.py:421
Async XLA Ops:
  1.7 0.9 %copy-start.3 = (f32[16,2048]{1,0:T(8,128)S(1)}, f32[16,2048]{1,0:T(8,128)}, u32[]{:S(2)}) copy-start(f32[16,2048]{1,0:T(8,128)} %param.6) | copy-start | bytes 393220
  1.9 1.2 %copy-start = (bf16[16,64,384]{2,1,0:T(8,128)(2,1)S(1)}, bf16[16,64,384]{2,1,0:T(8,128)(2,1)}, u32[]{:S(2)}) copy-start(bf16[16,64,384]{2,1,0:T(8,128)(2,1)} %param.7) | copy-start | bytes 2359300
  2.8 0.8 copy-start.1
  3.0 0.7 copy-start.2

commit v2 on v1

--- a/solution.py
+++ b/solution.py
@@ -31,7 +31,6 @@
 
     for at in range(len(tiles)):
         block, factors = tiles[at], columns(tiles[at], at)
-        outside = [columns(value, at) if i != at else None for i, value in enumerate(tiles)]
         for k in range(tile):
             inverse = 1.0 / factors[k][k : k + 1, :]
 
@@ -42,11 +41,12 @@
             block = eliminated(block)
             factors = factors[: k + 1] + [eliminated(value) for value in factors[k + 1 :]]
         tiles[at] = block
-        for i in range(len(tiles)):
+        for i in [*range(at + 1, len(tiles)), *range(at)]:
             if i != at:
                 value = tiles[i]
+                outer = columns(value, at)
                 for k in range(tile):
-                    value = value - outside[i][k] * block[k : k + 1, :]
+                    value = value - outer[k] * block[k : k + 1, :]
                 tiles[i] = value
     return jnp.concatenate(tiles, axis=0)
 
@@ -60,13 +60,13 @@
     leaves, subs, elems, slots,
     right_ref, guess_ref, couple_ref, lists_ref, near_ref,
     x_ref, r_ref,
-    ext, powers, high_ref, low_ref, table, packed_out, packed_in, partial, arrived, total,
+    ext_zero, ext_one, ext_two, powers, high_ref, low_ref, couple_in, table, packed_out, packed_in, partial, arrived, total, pieces, met, pooled, joined,
     halo_send, halo_recv, sum_send, sum_recv,
 ):
+    ext = (ext_zero, ext_one, ext_two)
     count = leaves * subs
-    share = WIDTH // count
+    share, portion = WIDTH // count, KEPT // subs
     pairs, wings = elems // 2, slots // 2
-    zero_at = elems + 2 * slots
     grp, leaf, sub = (lax.axis_index(name) for name in ("grp", "leaf", "sub"))
     me = leaf * subs + sub
     steps = [(far, near) for far in range(leaves) for near in range(subs)][1:]
@@ -93,6 +93,8 @@
     has_next = me < count - 1
     has_previous = me > 0
 
+    packed_in[...] = jnp.zeros_like(packed_in)
+
     barrier = pltpu.get_barrier_semaphore()
     for step in steps:
         pl.semaphore_signal(barrier, inc=1, device_id=place(step), device_id_type=MESH)
@@ -106,23 +108,23 @@
         return slice(pair * 2 * DOF, (pair + 1) * 2 * DOF)
 
     def put(side, pair, value):
-        ext[side, 2 * pair] = value.astype(jnp.bfloat16)
-        ext[side, 2 * pair + 1] = swapped(value).astype(jnp.bfloat16)
+        ext[side][2 * pair] = value.astype(jnp.bfloat16)
+        ext[side][2 * pair + 1] = swapped(value).astype(jnp.bfloat16)
 
     for side in range(3):
-        ext[side, elems:] = jnp.zeros((2 * slots + 2, RHS, 2 * DOF), jnp.bfloat16)
+        ext[side][elems:] = jnp.zeros((2, RHS, 2 * DOF), jnp.bfloat16)
     tail = (WIDTH + SSTEP * RHS, 2 * WIDTH)
     high_ref[tail[0] : tail[1]] = jnp.zeros((tail[1] - tail[0], pairs * 2 * DOF), jnp.bfloat16)
     low_ref[tail[0] : tail[1]] = jnp.zeros((tail[1] - tail[0], pairs * 2 * DOF), jnp.bfloat16)
     for element in range(elems):
         for face in range(FACES):
             near = near_ref[face, element]
-            at = jnp.where(near < 0, zero_at, near)
+            at = jnp.where((near < 0) | (near >= elems), elems, near)
             table[element * FACES + face] = at if face % 2 == 0 else at ^ 1
     for way in range(2):
         for slot in range(slots):
             listed = lists_ref[0, way, slot]
-            at = jnp.where(listed < 0, zero_at, listed)
+            at = jnp.where(listed < 0, elems, listed)
             table[elems * FACES + way * slots + slot] = at if slot % 2 == 0 else at ^ 1
     for pair in range(pairs):
         guess = guess_ref[:, lanes(pair)]
@@ -152,7 +154,7 @@
             for wing in range(wings):
                 at = elems * FACES + way * slots + 2 * wing
                 packed_out[side, way, wing] = jnp.where(
-                    half, ext[side, table[at]], ext[side, table[at + 1]]
+                    half, ext[side][table[at]], ext[side][table[at + 1]]
                 )
 
         pack(0)
@@ -171,14 +173,10 @@
         @pl.when(has_previous)
         def _():
             ahead(side).wait_recv()
-            for wing in range(wings):
-                put(side, pairs + wing, packed_in[side, 0, wing].astype(jnp.float32))
 
         @pl.when(has_next)
         def _():
             back(side).wait_recv()
-            for wing in range(wings):
-                put(side, pairs + wings + wing, packed_in[side, 1, wing].astype(jnp.float32))
 
         @pl.when(has_next)
         def _():
@@ -187,13 +185,30 @@
         @pl.when(has_previous)
         def _():
             back(side).wait_send()
+
+    def spread_couple():
+        shape = (FACES * DOF, 2 * slots * DOF)
+        slot_of = lax.broadcasted_iota(jnp.int32, (DOF, shape[1]), 1) // DOF
+        inner = lax.broadcasted_iota(jnp.int32, (DOF, shape[1]), 1) % DOF
+        same = inner == lax.broadcasted_iota(jnp.int32, (DOF, shape[1]), 0)
+        where_to = jnp.where(same, slot_of, -1 - 2 * elems)
+        for element in range(elems):
+            rows = slice(element * DOF, (element + 1) * DOF)
+            chosen = [
+                jnp.where(where_to == near_ref[face, element] - elems, 1.0, 0.0)
+                for face in range(FACES)
+            ]
+            chosen = jnp.concatenate(chosen, axis=0).astype(jnp.bfloat16)
+            couple_in[rows, :] = jnp.dot(
+                couple_ref[rows, :], chosen, preferred_element_type=jnp.float32
+            ).astype(jnp.bfloat16)
 
     def applied(side, pair):
         def gathered(element):
             blocks = []
             for face in range(0, FACES, 2):
                 at = element * FACES + face
-                blocks.append(jnp.where(half, ext[side, table[at]], ext[side, table[at + 1]]))
+                blocks.append(jnp.where(half, ext[side][table[at]], ext[side][table[at + 1]]))
             return jnp.concatenate(blocks, axis=1)
 
         both = jnp.concatenate([gathered(2 * pair), gathered(2 * pair + 1)], axis=0)
@@ -203,9 +218,23 @@
         )
         return jnp.where(half, image[:RHS], image[RHS:])
 
+    def prepare(side, order):
+        images = [applied(side, pair) for pair in range(pairs)]
+        for pair, image in enumerate(images):
+            powers[order, :, lanes(pair)] = image
+
+    def complete(side, order):
+        finish(side)
+        received = jnp.concatenate(
+            [packed_in[side, way, wing] for way in range(2) for wing in range(wings)], axis=1
+        )
+        more = lax.dot_general(
+            received, couple_in[...], (((1,), (1,)), ((), ())), preferred_element_type=jnp.float32
+        )
+        return [powers[order, :, lanes(pair)] + more[:, lanes(pair)] for pair in range(pairs)]
+
     def advance(side, order, store=True):
-        for pair in range(pairs):
-            image = applied(side, pair)
+        for pair, image in enumerate(complete(side, order)):
             powers[order, :, lanes(pair)] = image
             if store:
                 put((side + 1) % 3, pair, image)
@@ -222,17 +251,18 @@
     last = 2 * SSTEP
 
     begin(2)
-    finish(2)
-    for pair in range(pairs):
+    spread_couple()
+    prepare(2, 0)
+    for pair, image in enumerate(complete(2, 0)):
         at = lanes(pair)
-        first = right_ref[:, at] - guess_ref[:, at] + applied(2, pair)
+        first = right_ref[:, at] - guess_ref[:, at] + image
         powers[0, :, at] = first
         put(0, pair, first)
     begin(0)
     for pair in range(pairs):
         keep(last, powers[0, :, lanes(pair)], lanes(pair))
     for order in range(SSTEP):
-        finish(order)
+        prepare(order, order + 1)
         advance(order, order + 1)
         if order < SSTEP - 1:
             begin(order + 1)
@@ -256,17 +286,20 @@
     def gather():
         return sum_copy(total.at[rest], total.at[rest], steps[0], 1)
 
-    def begin_sum():
+    def gram_of(rows):
         def stacked(ref):
             return jnp.concatenate([ref[:KEPT], ref[last * RHS : (last + 1) * RHS]], axis=0)
 
         def product(left, right):
             return lax.dot_general(
-                left, right, (((1,), (1,)), ((), ())), preferred_element_type=jnp.float32
+                left[:rows], right, (((1,), (1,)), ((), ())), preferred_element_type=jnp.float32
             )
 
         high, low = stacked(high_ref), stacked(low_ref)
-        gram = product(high, high) + product(high, low) + product(low, high)
+        return product(high, high) + product(high, low) + product(low, high)
+
+    def begin_sum():
+        gram = gram_of(WIDTH)
         for shard in range(count):
             partial[shard] = gram[shard * share : (shard + 1) * share, :]
         for slot, step in enumerate(steps):
@@ -286,8 +319,44 @@
         gather().wait_recv()
         gather().wait_send()
 
-    def solved():
-        system = jnp.concatenate([total[shard] for shard in range(count)], axis=0)[:KEPT]
+    nearby = [(0, near) for near in range(1, subs)]
+    faraway = [(far, 0) for far in range(1, leaves)]
+
+    def last_sum():
+        gram = gram_of(KEPT)
+        for part in range(subs):
+            pieces[part] = gram[part * portion : (part + 1) * portion]
+        for slot, step in enumerate(nearby):
+            sum_copy(pieces.at[turned(sub, step[1], subs)], met.at[slot], step, 2).start()
+        swap = sum_copy(met, met, nearby[0], 2)
+        swap.wait_recv()
+        mine = pieces[sub]
+        for slot in range(subs - 1):
+            mine = mine + met[slot]
+        pooled[leaf] = mine
+        for step in faraway:
+            sum_copy(pooled.at[leaf], pooled.at[leaf], step, 3).start()
+        swap.wait_send()
+        others = pooled.at[pl.ds(1, leaves - 1)]
+        spread = sum_copy(others, others, faraway[0], 3)
+        spread.wait_recv()
+        mine = pooled[0]
+        for other in range(1, leaves):
+            mine = mine + pooled[other]
+        joined[sub] = mine
+        for step in nearby:
+            sum_copy(joined.at[sub], joined.at[sub], step, 4).start()
+        spread.wait_send()
+        others = joined.at[pl.ds(1, subs - 1)]
+        share_out = sum_copy(others, others, nearby[0], 4)
+        share_out.wait_recv()
+        share_out.wait_send()
+        return jnp.concatenate([joined[part] for part in range(subs)], axis=0)
+
+    def summed():
+        return jnp.concatenate([total[shard] for shard in range(count)], axis=0)[:KEPT]
+
+    def solved(system):
         whole = gauss_jordan(system)
         whole = jnp.concatenate([whole, jnp.zeros((RHS, WIDTH), jnp.float32)], axis=0)
         return whole.T[KEPT:]
@@ -335,18 +404,18 @@
     def cycle(repeat, carry):
         begin(0)
         begin_sum()
-        finish(0)
+        prepare(0, SSTEP + 1)
         advance(0, SSTEP + 1)
         begin(1)
         differ(SSTEP, SSTEP)
+        prepare(1, SSTEP + 2)
         turn_sum()
-        finish(1)
         advance(1, SSTEP + 2)
         begin(2)
         differ(SSTEP + 1, SSTEP + 1)
+        prepare(2, SSTEP + 3)
         finish_sum()
-        finish(2)
-        coeffs = solved()
+        coeffs = solved(summed())
         advance(2, SSTEP + 3, False)
         differ(SSTEP + 2, SSTEP + 2)
         parts = factors(coeffs, False)
@@ -367,10 +436,7 @@
         return carry
 
     lax.fori_loop(0, CYCLES - 1, cycle, 0)
-    begin_sum()
-    turn_sum()
-    finish_sum()
-    parts = factors(solved(), True)
+    parts = factors(solved(last_sum()), True)
     for at in spans:
         change = changes(parts, at)
         x_ref[:, at] = x_ref[:, at] + change[RHS:]
@@ -381,7 +447,7 @@
     elems, _, _ = couple.shape
     slots = send_lists.shape[2]
     count = leaves * subs
-    share = WIDTH // count
+    share, portion = WIDTH // count, KEPT // subs
     rows = elems * DOF
     vmem = pl.BlockSpec(memory_space=pltpu.VMEM)
     smem = pl.BlockSpec(memory_space=pltpu.SMEM)
@@ -396,20 +462,27 @@
         in_specs=[vmem, vmem, vmem, smem, smem],
         out_specs=(vmem, vmem),
         scratch_shapes=[
-            pltpu.VMEM((3, elems + 2 * slots + 2, RHS, 2 * DOF), jnp.bfloat16),
+            pltpu.VMEM((elems + 2, RHS, 2 * DOF), jnp.bfloat16),
+            pltpu.VMEM((elems + 2, RHS, 2 * DOF), jnp.bfloat16),
+            pltpu.VMEM((elems + 2, RHS, 2 * DOF), jnp.bfloat16),
             pltpu.VMEM((2 * SSTEP + 1, RHS, rows), jnp.float32),
             pltpu.VMEM((2 * WIDTH, rows), jnp.bfloat16),
             pltpu.VMEM((2 * WIDTH, rows), jnp.bfloat16),
+            pltpu.VMEM((rows, 2 * slots * DOF), jnp.bfloat16),
             pltpu.SMEM((elems * FACES + 2 * slots,), jnp.int32),
             pltpu.VMEM((3, 2, slots // 2, RHS, 2 * DOF), jnp.bfloat16),
             pltpu.VMEM((3, 2, slots // 2, RHS, 2 * DOF), jnp.bfloat16),
             pltpu.VMEM((count, share, WIDTH), jnp.float32),
             pltpu.VMEM((count, share, WIDTH), jnp.float32),
             pltpu.VMEM((count, share, WIDTH), jnp.float32),
+            pltpu.VMEM((subs, portion, WIDTH), jnp.float32),
+            pltpu.VMEM((subs - 1, portion, WIDTH), jnp.float32),
+            pltpu.VMEM((leaves, portion, WIDTH), jnp.float32),
+            pltpu.VMEM((subs, portion, WIDTH), jnp.float32),
             pltpu.SemaphoreType.DMA((3, 2)),
             pltpu.SemaphoreType.DMA((3, 2)),
-            pltpu.SemaphoreType.DMA((2,)),
-            pltpu.SemaphoreType.DMA((2,)),
+            pltpu.SemaphoreType.DMA((5,)),
+            pltpu.SemaphoreType.DMA((5,)),
         ],
         compiler_params=pltpu.CompilerParams(
             collective_id=0, has_side_effects=True, vmem_limit_bytes=40 * 1024 * 1024

time: 87.3 us -> 71.2 us (0.82)
  Pallas kernels: 81.3 us -> 65.1 us
    pallas_call x1, Pallas kernels: 81.3 us -> 65.1 us  [shards(): pl.pallas_call(functools.partial(kernel, leaves, subs, elems, slots), out...]
where the time goes in v2:
time: 71.2 us; the launch traced here: 71 us
  Pallas kernels  65.1 us (91%)
  local copies, waits for them, and re-layouts  5.19 us (7%)
    pallas_call x1, Pallas kernels, shards(): pl.pallas_call(functools.partial(kernel, leaves, subs, elems, slots), out...  65.1 us
    reshape x2, local copies, waits for them, and re-layouts, shards(): return (x.T.reshape(right_side.shape), r.T.reshape(right_side.shape))  1.79 us
    reshape x4, local copies, waits for them, and re-layouts, turned(): return value.reshape(rows, RHS).T  1.58 us
    unnamed x8, local copies, waits for them, and re-layouts  1.44 us

profile of v2, /device:TPU:0, one launch (start us, length us, event | category | flops | bytes accessed | tf_op | source)
XLA Modules:
  0.0 71.0 jit_solution(13793586778563469287)
XLA Ops:
  0.6 1.1 %reshape.19 = f32[1024,32]{1,0:T(8,128)S(1)} reshape(f32[16,2048]{1,0:T(8,128)} %param.5) | data formatting | bytes 262144 | tf_op jit(solution)/shard_map/reshape | solution.py:457
  1.7 0.0 copy-start.3
  1.7 0.2 copy.7
  1.9 0.0 copy-start
  1.9 0.7 %copy-done.3 = f32[16,2048]{1,0:T(8,128)S(1)} copy-done((f32[16,2048]{1,0:T(8,128)S(1)}, f32[16,2048]{1,0:T(8,128)}, u32[]{:S(2)}) %copy-start.3) | copy-done | bytes 131096
  2.6 0.2 reshape.20
  2.8 0.0 copy-start.1
  2.8 0.2 copy.8
  3.0 0.0 copy-start.2
  3.0 0.1 copy-done
  3.0 0.5 copy-done.1
  3.5 0.1 copy-done.2
  3.7 65.1 %shard_map.68 = (f32[32,1024]{1,0:T(8,128)S(1)}, f32[32,1024]{1,0:T(8,128)S(1)}) custom-call(f32[32,1024]{1,0:T(8,128)S(1)} %bitcast.7, f32[32,1024]{1,0:T(8,128)S(1)} %bitcast.8, bf16[1024,384]{1,0:T(8,128)(2,1)S(1)} %bitcast.6, s32[1,2,4]{2,1,0:T(2,128)S(1)} %copy-done.2, s32[6,16]{1,0:T(8,128)S(1)} %bitcast.11), custom_call_target="tpu_custom_call" | custom-call | tf_op jit(solution)/shard_map/pallas_call | solution.py:459
  68.8 0.2 copy.10
  69.0 0.9 %reshape.23 = f32[16,2048]{1,0:T(8,128)} reshape(f32[1024,32]{1,0:T(8,128)S(1)} %copy.10) | data formatting | bytes 262144 | tf_op jit(solution)/shard_map/reshape | solution.py:494
  69.9 0.2 copy.9
  70.1 0.9 %reshape.22 = f32[16,2048]{1,0:T(8,128)} reshape(f32[1024,32]{1,0:T(8,128)S(1)} %copy.9) | data formatting | bytes 262144 | tf_op jit(solution)/shard_map/reshape | solution.py:494
Async XLA Ops:
  1.7 0.9 %copy-start.3 = (f32[16,2048]{1,0:T(8,128)S(1)}, f32[16,2048]{1,0:T(8,128)}, u32[]{:S(2)}) copy-start(f32[16,2048]{1,0:T(8,128)} %param.6) | copy-start | bytes 393220
  1.9 1.2 %copy-start = (bf16[16,64,384]{2,1,0:T(8,128)(2,1)S(1)}, bf16[16,64,384]{2,1,0:T(8,128)(2,1)}, u32[]{:S(2)}) copy-start(bf16[16,64,384]{2,1,0:T(8,128)(2,1)} %param.7) | copy-start | bytes 2359300
  2.8 0.8 %copy-start.1 = (s32[16,6]{0,1:T(8,128)S(1)}, s32[16,6]{0,1:T(8,128)}, u32[]{:S(2)}) copy-start(s32[16,6]{0,1:T(8,128)} %param.9) | copy-start | bytes 1156
  3.0 0.7 copy-start.2

commit v3 on v2

--- a/solution.py
+++ b/solution.py
@@ -58,8 +58,9 @@
 
 def kernel(
     leaves, subs, elems, slots,
-    right_ref, guess_ref, couple_ref, lists_ref, near_ref,
-    x_ref, r_ref,
+    right_in, guess_in, couple_hbm, near_ref,
+    x_out, r_out,
+    x_ref, r_ref, right_raw, guess_raw, couple_ref, stage, loaded,
     ext_zero, ext_one, ext_two, powers, high_ref, low_ref, couple_in, table, packed_out, packed_in, partial, arrived, total, pieces, met, pooled, joined,
     halo_send, halo_recv, sum_send, sum_recv,
 ):
@@ -98,6 +99,15 @@
     barrier = pltpu.get_barrier_semaphore()
     for step in steps:
         pl.semaphore_signal(barrier, inc=1, device_id=place(step), device_id_type=MESH)
+
+    def load(source, target, at):
+        return pltpu.make_async_copy(source, target, loaded.at[at])
+
+    loads = [
+        load(guess_in, guess_raw, 0), load(couple_hbm, couple_ref, 1), load(right_in, right_raw, 2)
+    ]
+    for one in loads:
+        one.start()
 
     half = lax.broadcasted_iota(jnp.int32, (RHS, 2 * DOF), 1) < DOF
 
@@ -123,13 +133,34 @@
             table[element * FACES + face] = at if face % 2 == 0 else at ^ 1
     for way in range(2):
         for slot in range(slots):
-            listed = lists_ref[0, way, slot]
+            listed = near_ref[FACES, way * slots + slot]
             at = jnp.where(listed < 0, elems, listed)
             table[elems * FACES + way * slots + slot] = at if slot % 2 == 0 else at ^ 1
+    def turn_in(raw, target, at):
+        for degree in range(DOF):
+            stage[at, pl.ds(degree, elems, stride=DOF), :] = raw[
+                :, degree * RHS : (degree + 1) * RHS
+            ]
+        for pair in range(pairs):
+            target[:, lanes(pair)] = stage[at, lanes(pair), :].T
+
+    def turn_out(values, target, at):
+        for pair, value in enumerate(values):
+            stage[at, lanes(pair), :] = value.T
+        group = WIDTH // RHS
+        for first in range(0, DOF, group):
+            target[:, first * RHS : (first + group) * RHS] = jnp.concatenate(
+                [
+                    stage[at, pl.ds(degree, elems, stride=DOF), :]
+                    for degree in range(first, first + group)
+                ],
+                axis=1,
+            )
+
+    loads[0].wait()
+    turn_in(guess_raw, x_ref, 0)
     for pair in range(pairs):
-        guess = guess_ref[:, lanes(pair)]
-        x_ref[:, lanes(pair)] = guess
-        put(2, pair, guess)
+        put(2, pair, x_ref[:, lanes(pair)])
 
     pl.semaphore_wait(barrier, count - 1)
 
@@ -251,11 +282,14 @@
     last = 2 * SSTEP
 
     begin(2)
+    loads[1].wait()
     spread_couple()
     prepare(2, 0)
+    loads[2].wait()
+    turn_in(right_raw, r_ref, 1)
     for pair, image in enumerate(complete(2, 0)):
         at = lanes(pair)
-        first = right_ref[:, at] - guess_ref[:, at] + image
+        first = r_ref[:, at] - x_ref[:, at] + image
         powers[0, :, at] = first
         put(0, pair, first)
     begin(0)
@@ -437,10 +471,14 @@
 
     lax.fori_loop(0, CYCLES - 1, cycle, 0)
     parts = factors(solved(last_sum()), True)
+    ends = [[], []]
     for at in spans:
         change = changes(parts, at)
-        x_ref[:, at] = x_ref[:, at] + change[RHS:]
-        r_ref[:, at] = powers[0, :, at] - change[:RHS]
+        moved = x_ref[:, at] + change[RHS:], powers[0, :, at] - change[:RHS]
+        for end, value in zip(ends, moved):
+            end += [value[:, lanes(pair)] for pair in range(2)]
+    turn_out(ends[0], x_out, 0)
+    turn_out(ends[1], r_out, 1)
 
 
 def shards(leaves, subs, right_side, first_guess, couple, send_lists, neighbours):
@@ -451,17 +489,23 @@
     rows = elems * DOF
     vmem = pl.BlockSpec(memory_space=pltpu.VMEM)
     smem = pl.BlockSpec(memory_space=pltpu.SMEM)
-    field = jax.ShapeDtypeStruct((RHS, rows), jnp.float32)
-
-    def turned(value):
-        return value.reshape(rows, RHS).T
-
-    x, r = pl.pallas_call(
+    hbm = pl.BlockSpec(memory_space=pltpu.HBM)
+    lists = jnp.pad(send_lists.reshape(1, 2 * slots), ((0, 0), (0, elems - 2 * slots)))
+    numbers = jnp.concatenate([neighbours.T, lists], axis=0)
+    field = jax.ShapeDtypeStruct(right_side.shape, jnp.float32)
+    return pl.pallas_call(
         functools.partial(kernel, leaves, subs, elems, slots),
         out_shape=(field, field),
-        in_specs=[vmem, vmem, vmem, smem, smem],
+        in_specs=[hbm, hbm, hbm, smem],
         out_specs=(vmem, vmem),
         scratch_shapes=[
+            pltpu.VMEM((RHS, rows), jnp.float32),
+            pltpu.VMEM((RHS, rows), jnp.float32),
+            pltpu.VMEM(right_side.shape, jnp.float32),
+            pltpu.VMEM(right_side.shape, jnp.float32),
+            pltpu.VMEM((rows, FACES * DOF), jnp.bfloat16),
+            pltpu.VMEM((2, rows, RHS), jnp.float32),
+            pltpu.SemaphoreType.DMA((3,)),
             pltpu.VMEM((elems + 2, RHS, 2 * DOF), jnp.bfloat16),
             pltpu.VMEM((elems + 2, RHS, 2 * DOF), jnp.bfloat16),
             pltpu.VMEM((elems + 2, RHS, 2 * DOF), jnp.bfloat16),
@@ -485,13 +529,12 @@
             pltpu.SemaphoreType.DMA((5,)),
         ],
         compiler_params=pltpu.CompilerParams(
-            collective_id=0, has_side_effects=True, vmem_limit_bytes=40 * 1024 * 1024
+            collective_id=0, has_side_effects=True, vmem_limit_bytes=54900 * 1024
         ),
     )(
-        turned(right_side), turned(first_guess),
-        couple.reshape(rows, FACES * DOF), send_lists, neighbours.T,
+        right_side, first_guess,
+        couple.reshape(rows, FACES * DOF), numbers,
     )
-    return x.T.reshape(right_side.shape), r.T.reshape(right_side.shape)
 
 
 def solution(mesh):

time: 71.2 us -> 68.3 us (0.959)
  local copies, waits for them, and re-layouts: 5.19 us -> 2.08 us
    reshape x6 -> x1, local copies, waits for them, and re-layouts: 3.36 us -> 0.77 us  [shards(): send_lists.reshape(1, 2 * slots)]
    unnamed x8 -> x4, local copies, waits for them, and re-layouts: 1.44 us -> 1.32 us
where the time goes in v3:
time: 68.3 us; the launch traced here: 68.2 us
  Pallas kernels  65.4 us (96%)
  local copies, waits for them, and re-layouts  2.08 us (3%)
    pallas_call x1, Pallas kernels, shards(): pl.pallas_call(functools.partial(kernel, leaves, subs, elems, slots), out...  65.4 us

profile of v3, /device:TPU:0, one launch (start us, length us, event | category | flops | bytes accessed | tf_op | source)
XLA Modules:
  0.0 68.2 jit_solution(3269203268565966742)
XLA Ops:
  0.6 0.0 copy-start
  0.6 0.8 %reshape.11 = s32[1,8]{1,0:T(1,128)S(1)} reshape(s32[1,2,4]{2,1,0:T(2,128)} %param.8) | data formatting | bytes 64 | tf_op jit(solution)/shard_map/reshape | solution.py:493
  1.4 0.0 copy-done
  1.4 65.4 %shard_map.68 = (f32[16,2048]{1,0:T(8,128)S(1)}, f32[16,2048]{1,0:T(8,128)S(1)}) custom-call(f32[16,2048]{1,0:T(8,128)} %right_in.1, f32[16,2048]{1,0:T(8,128)} %guess_in.1, bf16[1024,384]{1,0:T(8,128)(2,1)} %bitcast.2, s32[7,16]{1,0:T(8,128)S(1)} %pad_add_fusion.near_ref), custom_call_target="tpu_custom_call" | custom-call | tf_op jit(solution)/shard_map/pallas_call | solution.py:496
  66.9 0.7 copy.9
  67.5 0.7 copy.10
  (1 shorter events, 0.0 us)
Async XLA Ops:
  0.6 0.8 %copy-start = (s32[16,6]{0,1:T(8,128)S(1)}, s32[16,6]{0,1:T(8,128)}, u32[]{:S(2)}) copy-start(s32[16,6]{0,1:T(8,128)} %param.9) | copy-start | bytes 1156

commit v4 on v3

--- a/solution.py
+++ b/solution.py
@@ -67,10 +67,12 @@
     ext = (ext_zero, ext_one, ext_two)
     count = leaves * subs
     share, portion = WIDTH // count, KEPT // subs
+    needed = KEPT // share
     pairs, wings = elems // 2, slots // 2
     grp, leaf, sub = (lax.axis_index(name) for name in ("grp", "leaf", "sub"))
     me = leaf * subs + sub
-    steps = [(far, near) for far in range(leaves) for near in range(subs)][1:]
+    middle = sorted(range(leaves), key=lambda far: abs(far - leaves // 2))
+    steps = [step for step in [(far, near) for near in range(subs) for far in middle] if any(step)]
 
     def turned(value, step, size):
         moved = value + step
@@ -312,13 +314,15 @@
             device_id_type=MESH,
         )
 
-    rest = pl.ds(1, count - 1)
-
-    def scatter():
-        return sum_copy(partial.at[rest], arrived.at[rest], steps[0], 0)
-
-    def gather():
-        return sum_copy(total.at[rest], total.at[rest], steps[0], 1)
+    summing = me < needed
+
+    def scatter(blocks):
+        some = pl.ds(0, blocks)
+        return sum_copy(partial.at[some], arrived.at[some], steps[0], 0)
+
+    def gather(blocks):
+        some = pl.ds(0, blocks)
+        return sum_copy(total.at[some], total.at[some], steps[0], 1)
 
     def gram_of(rows):
         def stacked(ref):
@@ -333,25 +337,41 @@
         return product(high, high) + product(high, low) + product(low, high)
 
     def begin_sum():
-        gram = gram_of(WIDTH)
-        for shard in range(count):
+        gram = gram_of(KEPT)
+        for shard in range(needed):
             partial[shard] = gram[shard * share : (shard + 1) * share, :]
         for slot, step in enumerate(steps):
-            sum_copy(partial.at[peer(step)], arrived.at[slot + 1], step, 0).start()
+            to = peer(step)
+
+            @pl.when(to < needed)
+            def _(to=to, slot=slot, step=step):
+                sum_copy(partial.at[to], arrived.at[slot + 1], step, 0).start()
 
     def turn_sum():
-        scatter().wait_recv()
-        reduced = partial[me]
-        for step in range(1, count):
-            reduced = reduced + arrived[step]
-        total[me] = reduced
-        for step in steps:
-            sum_copy(total.at[me], total.at[me], step, 1).start()
-        scatter().wait_send()
+        @pl.when(summing)
+        def _():
+            scatter(count - 1).wait_recv()
+            reduced = partial[me]
+            for step in range(1, count):
+                reduced = reduced + arrived[step]
+            total[me] = reduced
+            for step in steps:
+                sum_copy(total.at[me], total.at[me], step, 1).start()
+            scatter(needed - 1).wait_send()
+
+        @pl.when(jnp.logical_not(summing))
+        def _():
+            scatter(needed).wait_send()
 
     def finish_sum():
-        gather().wait_recv()
-        gather().wait_send()
+        @pl.when(summing)
+        def _():
+            gather(needed - 1).wait_recv()
+            gather(count - 1).wait_send()
+
+        @pl.when(jnp.logical_not(summing))
+        def _():
+            gather(needed).wait_recv()
 
     nearby = [(0, near) for near in range(1, subs)]
     faraway = [(far, 0) for far in range(1, leaves)]
@@ -388,7 +408,7 @@
         return jnp.concatenate([joined[part] for part in range(subs)], axis=0)
 
     def summed():
-        return jnp.concatenate([total[shard] for shard in range(count)], axis=0)[:KEPT]
+        return jnp.concatenate([total[shard] for shard in range(needed)], axis=0)
 
     def solved(system):
         whole = gauss_jordan(system)
@@ -481,6 +501,17 @@
     turn_out(ends[1], r_out, 1)
 
 
+def hand_over(x_ref, r_ref, x_out, r_out, moved):
+    copies = [
+        pltpu.make_async_copy(source, target, moved.at[at])
+        for at, (source, target) in enumerate([(x_ref, x_out), (r_ref, r_out)])
+    ]
+    for copy in copies:
+        copy.start()
+    for copy in copies:
+        copy.wait()
+
+
 def shards(leaves, subs, right_side, first_guess, couple, send_lists, neighbours):
     elems, _, _ = couple.shape
     slots = send_lists.shape[2]
@@ -493,7 +524,7 @@
     lists = jnp.pad(send_lists.reshape(1, 2 * slots), ((0, 0), (0, elems - 2 * slots)))
     numbers = jnp.concatenate([neighbours.T, lists], axis=0)
     field = jax.ShapeDtypeStruct(right_side.shape, jnp.float32)
-    return pl.pallas_call(
+    ends = pl.pallas_call(
         functools.partial(kernel, leaves, subs, elems, slots),
         out_shape=(field, field),
         in_specs=[hbm, hbm, hbm, smem],
@@ -535,6 +566,14 @@
         right_side, first_guess,
         couple.reshape(rows, FACES * DOF), numbers,
     )
+    return pl.pallas_call(
+        hand_over,
+        out_shape=(field, field),
+        in_specs=[vmem, vmem],
+        out_specs=(hbm, hbm),
+        scratch_shapes=[pltpu.SemaphoreType.DMA((2,))],
+        compiler_params=pltpu.CompilerParams(vmem_limit_bytes=1024 * 1024),
+    )(*ends)
 
 
 def solution(mesh):

time: 68.3 us -> 66.6 us (0.975)
  local copies, waits for them, and re-layouts: 2.08 us -> 0.77 us
    unnamed x4 -> x2, local copies, waits for them, and re-layouts: 1.32 us -> 0.01 us
    pallas_call x1, Pallas kernels: 65.4 us -> 64.2 us  [shards(): pl.pallas_call(functools.partial(kernel, leaves, subs, elems, slots), out...]
    pallas_call x0 -> x1, Pallas kernels: none -> 0.72 us  [shards(): pl.pallas_call(hand_over, out_shape=(field, field), in_specs=[vmem, vmem]...]
where the time goes in v4:
time: 66.6 us; the launch traced here: 66.3 us
  Pallas kernels  64.9 us (97%)
  local copies, waits for them, and re-layouts  0.77 us (1%)
    pallas_call x1, Pallas kernels, shards(): pl.pallas_call(functools.partial(kernel, leaves, subs, elems, slots), out...  64.2 us

profile of v4, /device:TPU:0, one launch (start us, length us, event | category | flops | bytes accessed | tf_op | source)
XLA Modules:
  0.0 66.3 jit_solution(12850580392678701933)
XLA Ops:
  0.6 0.0 copy-start
  0.6 0.8 %reshape.11 = s32[1,8]{1,0:T(1,128)S(1)} reshape(s32[1,2,4]{2,1,0:T(2,128)} %param.8) | data formatting | bytes 64 | tf_op jit(solution)/shard_map/reshape | solution.py:524
  1.4 0.0 copy-done
  1.4 64.2 %shard_map.68 = (f32[16,2048]{1,0:T(8,128)S(1)}, f32[16,2048]{1,0:T(8,128)S(1)}) custom-call(f32[16,2048]{1,0:T(8,128)} %right_in.1, f32[16,2048]{1,0:T(8,128)} %guess_in.1, bf16[1024,384]{1,0:T(8,128)(2,1)} %bitcast.2, s32[7,16]{1,0:T(8,128)S(1)} %pad_add_fusion.near_ref), custom_call_target="tpu_custom_call" | custom-call | tf_op jit(solution)/shard_map/pallas_call | solution.py:527
  65.6 0.7 %shard_map.69 = (f32[16,2048]{1,0:T(8,128)}, f32[16,2048]{1,0:T(8,128)}) custom-call(f32[16,2048]{1,0:T(8,128)S(1)} %get-tuple-element.4.x_ref, f32[16,2048]{1,0:T(8,128)S(1)} %get-tuple-element.5.r_ref), custom_call_target="tpu_custom_call" | custom-call | tf_op jit(solution)/shard_map/pallas_call | solution.py:569
  (1 shorter events, 0.0 us)
Async XLA Ops:
  0.6 0.8 %copy-start = (s32[16,6]{0,1:T(8,128)S(1)}, s32[16,6]{0,1:T(8,128)}, u32[]{:S(2)}) copy-start(s32[16,6]{0,1:T(8,128)} %param.9) | copy-start | bytes 1156

commit v5 on v4

--- a/solution.py
+++ b/solution.py
@@ -333,8 +333,8 @@
                 left[:rows], right, (((1,), (1,)), ((), ())), preferred_element_type=jnp.float32
             )
 
-        high, low = stacked(high_ref), stacked(low_ref)
-        return product(high, high) + product(high, low) + product(low, high)
+        high = stacked(high_ref)
+        return product(high, high)
 
     def begin_sum():
         gram = gram_of(KEPT)
@@ -461,9 +461,9 @@
         prepare(0, SSTEP + 1)
         advance(0, SSTEP + 1)
         begin(1)
-        differ(SSTEP, SSTEP)
         prepare(1, SSTEP + 2)
         turn_sum()
+        differ(SSTEP, SSTEP)
         advance(1, SSTEP + 2)
         begin(2)
         differ(SSTEP + 1, SSTEP + 1)

time: 66.6 us -> 65.9 us (0.989)
  Pallas kernels: 64.9 us -> 64.1 us
    pallas_call x1, Pallas kernels: 64.2 us -> 63.4 us  [shards(): pl.pallas_call(functools.partial(kernel, leaves, subs, elems, slots), out...]
where the time goes in v5:
time: 65.9 us; the launch traced here: 65.5 us
  Pallas kernels  64.1 us (97%)
  local copies, waits for them, and re-layouts  0.77 us (1%)
    pallas_call x1, Pallas kernels, shards(): pl.pallas_call(functools.partial(kernel, leaves, subs, elems, slots), out...  63.4 us

profile of v5, /device:TPU:0, one launch (start us, length us, event | category | flops | bytes accessed | tf_op | source)
XLA Modules:
  0.0 65.5 jit_solution(1911500515083942589)
XLA Ops:
  0.6 0.0 copy-start
  0.6 0.8 %reshape.11 = s32[1,8]{1,0:T(1,128)S(1)} reshape(s32[1,2,4]{2,1,0:T(2,128)} %param.8) | data formatting | bytes 64 | tf_op jit(solution)/shard_map/reshape | solution.py:524
  1.4 0.0 copy-done
  1.4 63.4 %shard_map.68 = (f32[16,2048]{1,0:T(8,128)S(1)}, f32[16,2048]{1,0:T(8,128)S(1)}) custom-call(f32[16,2048]{1,0:T(8,128)} %right_in.1, f32[16,2048]{1,0:T(8,128)} %guess_in.1, bf16[1024,384]{1,0:T(8,128)(2,1)} %bitcast.2, s32[7,16]{1,0:T(8,128)S(1)} %pad_add_fusion.near_ref), custom_call_target="tpu_custom_call" | custom-call | tf_op jit(solution)/shard_map/pallas_call | solution.py:527
  64.8 0.7 %shard_map.69 = (f32[16,2048]{1,0:T(8,128)}, f32[16,2048]{1,0:T(8,128)}) custom-call(f32[16,2048]{1,0:T(8,128)S(1)} %get-tuple-element.4.x_ref, f32[16,2048]{1,0:T(8,128)S(1)} %get-tuple-element.5.r_ref), custom_call_target="tpu_custom_call" | custom-call | tf_op jit(solution)/shard_map/pallas_call | solution.py:569
  (1 shorter events, 0.0 us)
Async XLA Ops:
  0.6 0.8 %copy-start = (s32[16,6]{0,1:T(8,128)S(1)}, s32[16,6]{0,1:T(8,128)}, u32[]{:S(2)}) copy-start(s32[16,6]{0,1:T(8,128)} %param.9) | copy-start | bytes 1156
